TPU v7x, 32 devices: a whole 2x2x4 slice. The times are simulated.
32 devices in a mesh: batch: 4 (over y, x), head: 8 (over z, core).
Axes of the slice: x: 2, y: 2, z: 4, core: 2. Of those that a mesh axis runs over, the one named last changes fastest.
Arguments:
- tokens: bfloat16 [8, 1024, 2048], P('batch', 'head'), may hold values from -6 to 6
- segment_ids: int32 [8, 1024], P('batch'), may hold values from 0 to 3, as said below
- position_ids: int32 [8, 1024], P('batch'), may hold values from 0 to 1023, as said below
- w_query: bfloat16 [2048, 2048], P('batch', 'head'), may hold values from -0.125 to 0.125
- w_key: bfloat16 [2048, 2048], P('batch', 'head'), may hold values from -0.125 to 0.125
- w_value: bfloat16 [2048, 2048], P('batch', 'head'), may hold values from -0.125 to 0.125
- w_output: bfloat16 [2048, 2048], P('batch', 'head'), may hold values from -0.75 to 0.75
- w_gate: bfloat16 [2048, 8192], P('batch', 'head'), may hold values from -0.125 to 0.125
- w_up: bfloat16 [2048, 8192], P('batch', 'head'), may hold values from -0.125 to 0.125
- w_down: bfloat16 [2048, 8192], P('batch', 'head'), may hold values from -0.0625 to 0.0625
- attn_gain: bfloat16 [2048], P('batch'), may hold values from 0.099609375 to 1.8984375
- mlp_gain: bfloat16 [2048], P('batch'), may hold values from 0.099609375 to 1.8984375
- cotangent: bfloat16 [8, 1024, 2048], P('batch', 'head'), may hold values from -6 to 6
Outputs:
- layer_out: bfloat16 [8, 1024, 2048], P('batch', 'head')
- grad_input: float32 [8, 1024, 2048], P('batch', 'head')
- grad_query: float32 [2048, 2048], P('batch', 'head')
- grad_key: float32 [2048, 2048], P('batch', 'head')
- grad_value: float32 [2048, 2048], P('batch', 'head')
- grad_output: float32 [2048, 2048], P('batch', 'head')
- grad_gate: float32 [2048, 8192], P('batch', 'head')
- grad_up: float32 [2048, 8192], P('batch', 'head')
- grad_down: float32 [2048, 8192], P('batch', 'head')
- grad_attn_gain: float32 [2048], P('batch')
- grad_mlp_gain: float32 [2048], P('batch')
Inputs may be any that keep to these rules, and one draw needn't show every extreme that they name: `segment_ids`: within a row the ids start at 0, rise by one at each document's first token and never fall. In every aligned block of 2 rows, one row (which one is drawn from the seed) is a single document of all 1024 tokens, and the next row in the block (cyclically) is cut into documents of exactly 256 tokens; in all other rows documents have 256 to 512 tokens except the last of a row, which may be shorter. `position_ids`: the token's index counted from its document's first token.
All inputs are finite; a program needn't handle non-finite values.
Results may differ from a plain program's by a relative error of at most 0.02.
Values may be sent and summed in bfloat16 or wider, within the bound.
A program may use at most 184 MiB of HBM per device.

v0:
```python
import jax
import jax.numpy as jnp
from jax import lax
from jax.sharding import PartitionSpec as P

HEAD_DIM = 64
epsilon = 1e-05
rope_base = 130000.0
masked_value = -1000000000.0


def normed(values, gain):
    inv_root = lax.rsqrt(jnp.mean(values * values, axis=-1, keepdims=True) + epsilon)
    return values * inv_root * gain


def norm_back(values, gain, grad):
    inv_root = lax.rsqrt(jnp.mean(values * values, axis=-1, keepdims=True) + epsilon)
    unit = values * inv_root
    weighted = grad * gain
    grad_values = inv_root * (weighted - unit * jnp.mean(weighted * unit, axis=-1, keepdims=True))
    return (grad_values, grad * unit)


def rope_tables(positions):
    half_dim = HEAD_DIM // 2
    frequency = rope_base ** (-(jnp.arange(half_dim).astype(jnp.float32) * 2.0) / HEAD_DIM)
    angles = positions.astype(jnp.float32)[:, None] * frequency[None, :]
    return (jnp.cos(angles)[:, None, :], jnp.sin(angles)[:, None, :])


def rotate(values, cosine, sine):
    half_dim = values.shape[-1] // 2
    first_half = values[..., :half_dim]
    second = values[..., half_dim:]
    return jnp.concatenate(
        [first_half * cosine - second * sine, second * cosine + first_half * sine], axis=-1
    )


def contract_rows(left, right):
    return lax.dot_general(
        left, right, (((0,), (0,)), ((), ())), preferred_element_type=jnp.float32
    )


def contract_cols(left, right):
    return lax.dot_general(
        left, right, (((1,), (1,)), ((), ())), preferred_element_type=jnp.float32
    )


def fetch_weights(w_query, w_key, w_value, w_output, w_gate, w_up, w_down, attn_gain, mlp_gain):
    return (
        lax.all_gather(w_query, "batch", axis=0, tiled=True),
        lax.all_gather(w_key, "batch", axis=0, tiled=True),
        lax.all_gather(w_value, "batch", axis=0, tiled=True),
        lax.all_gather(w_output, "batch", axis=0, tiled=True),
        lax.all_gather(w_gate, "batch", axis=0, tiled=True),
        lax.all_gather(w_up, "batch", axis=0, tiled=True),
        lax.all_gather(w_down, "batch", axis=0, tiled=True),
        lax.all_gather(attn_gain, "batch", axis=0, tiled=True),
        lax.all_gather(mlp_gain, "batch", axis=0, tiled=True),
    )


def reduce_grads(grad_parts):
    gain_sums = lax.psum((grad_parts[7], grad_parts[8]), "head")
    return (
        lax.psum_scatter(
            grad_parts[0].astype(jnp.bfloat16), "batch", scatter_dimension=0, tiled=True
        ).astype(jnp.float32),
        lax.psum_scatter(
            grad_parts[1].astype(jnp.bfloat16), "batch", scatter_dimension=0, tiled=True
        ).astype(jnp.float32),
        lax.psum_scatter(
            grad_parts[2].astype(jnp.bfloat16), "batch", scatter_dimension=0, tiled=True
        ).astype(jnp.float32),
        lax.psum_scatter(
            grad_parts[3].astype(jnp.bfloat16), "batch", scatter_dimension=0, tiled=True
        ).astype(jnp.float32),
        lax.psum_scatter(
            grad_parts[4].astype(jnp.bfloat16), "batch", scatter_dimension=0, tiled=True
        ).astype(jnp.float32),
        lax.psum_scatter(
            grad_parts[5].astype(jnp.bfloat16), "batch", scatter_dimension=0, tiled=True
        ).astype(jnp.float32),
        lax.psum_scatter(
            grad_parts[6].astype(jnp.bfloat16), "batch", scatter_dimension=0, tiled=True
        ).astype(jnp.float32),
        lax.psum_scatter(
            gain_sums[0].astype(jnp.bfloat16), "batch", scatter_dimension=0, tiled=True
        ).astype(jnp.float32),
        lax.psum_scatter(
            gain_sums[1].astype(jnp.bfloat16), "batch", scatter_dimension=0, tiled=True
        ).astype(jnp.float32),
    )


def block_scores(query, key_rot, segments, block_start):
    block_len = query.shape[0]
    scores = jnp.einsum(
        "qhd,khd->hqk", query, key_rot, preferred_element_type=jnp.float32
    ) * HEAD_DIM ** (-0.5)
    query_index = block_start + jnp.arange(block_len)[:, None]
    key_index = jnp.arange(key_rot.shape[0])[None, :]
    same_doc = segments[block_start : block_start + block_len][:, None] == segments[None, :]
    return (scores, (same_doc & (key_index <= query_index))[None, :, :])


def attend_forward(query, key_rot, values, segments):
    length = query.shape[0]
    block_len = min(512, length)
    results = []
    log_sums = []
    for block_start in range(0, length, block_len):
        scores, allowed = block_scores(
            query[block_start : block_start + block_len], key_rot, segments, block_start
        )
        masked = jnp.where(allowed, scores, masked_value)
        row_max = jnp.max(masked, axis=-1, keepdims=True)
        weights_exp = jnp.exp(masked - row_max)
        row_total = jnp.sum(weights_exp, axis=-1, keepdims=True)
        probabilities = (weights_exp / row_total).astype(jnp.bfloat16)
        results.append(
            jnp.einsum("hqk,khd->qhd", probabilities, values, preferred_element_type=jnp.float32)
        )
        log_sums.append(row_max + jnp.log(row_total))
    return (jnp.concatenate(results, axis=0), log_sums)


def attend_backward(query, key_rot, values, segments, log_sums, grad_out):
    length = query.shape[0]
    block_len = min(512, length)
    inv_scale = HEAD_DIM ** (-0.5)
    query_grads = []
    key_grad = jnp.zeros(key_rot.shape, jnp.float32)
    value_grad = jnp.zeros(values.shape, jnp.float32)
    for block_number, block_start in enumerate(range(0, length, block_len)):
        query_block = query[block_start : block_start + block_len]
        scores, allowed = block_scores(query_block, key_rot, segments, block_start)
        probs_full = jnp.exp(jnp.where(allowed, scores, masked_value) - log_sums[block_number])
        grad_block = grad_out[block_start : block_start + block_len]
        grad_prob = jnp.einsum(
            "qhd,khd->hqk", grad_block, values, preferred_element_type=jnp.float32
        )
        row_delta = jnp.sum(probs_full * grad_prob, axis=-1, keepdims=True)
        grad_score = (probs_full * (grad_prob - row_delta)).astype(jnp.bfloat16)
        query_grads.append(
            jnp.einsum("hqk,khd->qhd", grad_score, key_rot, preferred_element_type=jnp.float32)
            * inv_scale
        )
        key_grad = (
            key_grad
            + jnp.einsum(
                "hqk,qhd->khd", grad_score, query_block, preferred_element_type=jnp.float32
            )
            * inv_scale
        )
        value_grad = value_grad + jnp.einsum(
            "hqk,qhd->khd",
            probs_full.astype(jnp.bfloat16),
            grad_block,
            preferred_element_type=jnp.float32,
        )
    return (jnp.concatenate(query_grads, axis=0), key_grad, value_grad)


def per_device(
    tokens,
    segment_ids,
    position_ids,
    w_query,
    w_key,
    w_value,
    w_output,
    w_gate,
    w_up,
    w_down,
    attn_gain,
    mlp_gain,
    cotangent,
):
    row_count = tokens.shape[0]
    local_len = tokens.shape[1]
    offset = lax.axis_index("head") * local_len
    accumulated = None
    outputs = []
    input_grads = []
    for row_index in range(row_count):
        gathered = fetch_weights(
            w_query, w_key, w_value, w_output, w_gate, w_up, w_down, attn_gain, mlp_gain
        )
        query_w, key_w, value_w, output_w, gate_w, up_w, down_w = gathered[:7]
        gain_one = gathered[7].astype(jnp.float32)
        gain_two = gathered[8].astype(jnp.float32)
        segments = segment_ids[row_index]
        cosine, sine = rope_tables(position_ids[row_index])
        inputs = tokens[row_index].astype(jnp.float32)
        attn_in = lax.all_gather(
            normed(inputs, gain_one).astype(jnp.bfloat16), "head", axis=0, tiled=True
        )
        length = attn_in.shape[0]
        heads_here = query_w.shape[1] // HEAD_DIM
        head_shape = (length, heads_here, HEAD_DIM)
        query_lin = jnp.dot(attn_in, query_w, preferred_element_type=jnp.float32).reshape(
            head_shape
        )
        key_lin = jnp.dot(attn_in, key_w, preferred_element_type=jnp.float32).reshape(head_shape)
        query = rotate(query_lin, cosine, sine).astype(jnp.bfloat16)
        key_rot = rotate(key_lin, cosine, sine).astype(jnp.bfloat16)
        values = (
            jnp.dot(attn_in, value_w, preferred_element_type=jnp.float32)
            .astype(jnp.bfloat16)
            .reshape(head_shape)
        )
        attended, log_sums = attend_forward(query, key_rot, values, segments)
        attended = attended.reshape(length, heads_here * HEAD_DIM).astype(jnp.bfloat16)
        attn_terms = contract_cols(attended, output_w)
        token_rows = jnp.arange(length)
        own_rows = (token_rows >= offset) & (token_rows < offset + local_len)
        placed = lax.dynamic_update_slice_in_dim(jnp.zeros_like(attn_terms), inputs, offset, 0)
        mixed_full = lax.psum(attn_terms + placed, "head")
        mixed = lax.dynamic_slice_in_dim(mixed_full, offset, local_len, 0)
        mlp_in = normed(mixed_full, gain_two).astype(jnp.bfloat16)
        gate_act = jnp.dot(mlp_in, gate_w, preferred_element_type=jnp.float32)
        up_act = jnp.dot(mlp_in, up_w, preferred_element_type=jnp.float32)
        hidden = (jax.nn.silu(gate_act) * up_act).astype(jnp.bfloat16)
        mlp_terms = contract_cols(hidden, down_w)
        result = mixed + lax.psum_scatter(
            mlp_terms.astype(jnp.bfloat16), "head", scatter_dimension=0, tiled=True
        ).astype(jnp.float32)
        outputs.append(result.astype(jnp.bfloat16))
        grad_row = cotangent[row_index]
        grad_full = lax.all_gather(grad_row, "head", axis=0, tiled=True)
        grad_down = contract_rows(grad_full, hidden)
        grad_hidden = jnp.dot(grad_full, down_w, preferred_element_type=jnp.float32)
        _, pull_swish = jax.vjp(
            lambda gate_in, up_in: jax.nn.silu(gate_in) * up_in, gate_act, up_act
        )
        grad_gate_act, grad_up_act = pull_swish(grad_hidden)
        grad_gate_act = grad_gate_act.astype(jnp.bfloat16)
        grad_up_act = grad_up_act.astype(jnp.bfloat16)
        grad_gate = contract_rows(mlp_in, grad_gate_act)
        grad_up = contract_rows(mlp_in, grad_up_act)
        mlp_in_terms = contract_cols(grad_gate_act, gate_w) + contract_cols(grad_up_act, up_w)
        grad_mlp_in = lax.psum(mlp_in_terms, "head")
        grad_from_norm, gain_terms = norm_back(mixed_full, gain_two, grad_mlp_in)
        gain_two_grad = jnp.sum(jnp.where(own_rows[:, None], gain_terms, 0.0), axis=0)
        grad_mixed_full = grad_full.astype(jnp.float32) + grad_from_norm
        grad_mixed = lax.dynamic_slice_in_dim(grad_mixed_full, offset, local_len, 0)
        grad_att = grad_mixed_full.astype(jnp.bfloat16)
        grad_output = contract_rows(grad_att, attended)
        grad_attended = (
            jnp.dot(grad_att, output_w, preferred_element_type=jnp.float32)
            .astype(jnp.bfloat16)
            .reshape(head_shape)
        )
        query_rot_grad, key_rot_grad, value_rot_grad = attend_backward(
            query, key_rot, values, segments, log_sums, grad_attended
        )
        _, pull_rope = jax.vjp(
            lambda query_in, key_in: (rotate(query_in, cosine, sine), rotate(key_in, cosine, sine)),
            query_lin,
            key_lin,
        )
        query_pre_grad, key_pre_grad = pull_rope((query_rot_grad, key_rot_grad))
        query_grad_b = query_pre_grad.reshape(length, heads_here * HEAD_DIM).astype(jnp.bfloat16)
        key_grad_b = key_pre_grad.reshape(length, heads_here * HEAD_DIM).astype(jnp.bfloat16)
        value_grad_b = value_rot_grad.reshape(length, heads_here * HEAD_DIM).astype(jnp.bfloat16)
        grad_query = contract_rows(attn_in, query_grad_b)
        grad_key = contract_rows(attn_in, key_grad_b)
        grad_value = contract_rows(attn_in, value_grad_b)
        attn_in_terms = (
            contract_cols(query_grad_b, query_w)
            + contract_cols(key_grad_b, key_w)
            + contract_cols(value_grad_b, value_w)
        )
        grad_attn_in = lax.psum_scatter(
            attn_in_terms.astype(jnp.bfloat16), "head", scatter_dimension=0, tiled=True
        ).astype(jnp.float32)
        grad_from_first, first_terms = norm_back(inputs, gain_one, grad_attn_in)
        input_grads.append(grad_mixed + grad_from_first)
        grad_parts = (
            grad_query,
            grad_key,
            grad_value,
            grad_output,
            grad_gate,
            grad_up,
            grad_down,
            jnp.sum(first_terms, axis=0),
            gain_two_grad,
        )
        if accumulated is None:
            accumulated = grad_parts
        else:
            accumulated = jax.tree.map(jnp.add, accumulated, grad_parts)
    reduced = reduce_grads(accumulated)
    return (
        jnp.stack(outputs),
        jnp.stack(input_grads),
        reduced[0],
        reduced[1],
        reduced[2],
        reduced[3],
        reduced[4],
        reduced[5],
        reduced[6],
        reduced[7],
        reduced[8],
    )


def solution(mesh):
    placed = (
        P("batch", "head", None),
        P("batch", None),
        P("batch", None),
        P("batch", "head"),
        P("batch", "head"),
        P("batch", "head"),
        P("batch", "head"),
        P("batch", "head"),
        P("batch", "head"),
        P("batch", "head"),
        P("batch"),
        P("batch"),
        P("batch", "head", None),
    )
    return jax.shard_map(
        per_device,
        mesh=mesh,
        in_specs=placed,
        out_specs=(
            P("batch", "head", None),
            P("batch", "head", None),
            P("batch", "head"),
            P("batch", "head"),
            P("batch", "head"),
            P("batch", "head"),
            P("batch", "head"),
            P("batch", "head"),
            P("batch", "head"),
            P("batch"),
            P("batch"),
        ),
        check_vma=False,
    )
```

profile of v0, /device:TPU:0, one launch (start us, length us, event | category | flops | bytes accessed | tf_op | source)
XLA Modules:
  0.0 1740.3 jit_solution(4648591317237889378)
XLA Ops:
  39.2 49.3 %all-gather.32.cloned.1.call-done = bf16[1024,2048]{1,0:T(8,128)(2,1)} async-done(((bf16[128,2048]{1,0:T(8,128)(2,1)}), bf16[1024,2048]{1,0:T(8,128)(2,1)}) %all-gather.32.cloned.1.call-update) | async-done | bytes 4194320 | tf_op jit(solution)/shard_map/all_gather | solution.py:200
  92.4 23.4 %all-gather.20.cloned.1.call-done = bf16[2048,256]{1,0:T(8,128)(2,1)} async-done(((bf16[512,256]{1,0:T(8,128)(2,1)}), bf16[2048,256]{1,0:T(8,128)(2,1)}) %all-gather.20.cloned.1.call-update) | async-done | bytes 1048592 | tf_op jit(solution)/shard_map/all_gather | solution.py:55
  129.6 14.5 all-gather.18.cloned.1.call-done
  154.4 13.6 fusion.101
  168.0 25.3 %all-gather.16.cloned.1.call-done = bf16[1024,2048]{1,0:T(8,128)(2,1)} async-done(((bf16[128,2048]{1,0:T(8,128)(2,1)}), bf16[1024,2048]{1,0:T(8,128)(2,1)}) %all-gather.16.cloned.1.call-update) | async-done | bytes 4194320 | tf_op jit(solution)/shard_map/all_gather | solution.py:200
  246.4 321.8 %all-reduce.19.cloned.1.call-done = (f32[1024,2048]{1,0:T(8,128)}, f32[1024,2048]{1,0:T(8,128)}) async-done(((f32[1024,2048]{1,0:T(8,128)}, f32[1024,2048]{1,0:T(8,128)}), (f32[1024,2048]{1,0:T(8,128)}, f32[1024,2048]{1,0:T(8,128)})) %all-reduce.19.cloned.1.call-update) | async-done | bytes 16777232 | tf_op jit(solution)/shard_map/psum | solution.py:223
  581.2 41.7 %all-gather.28.cloned.1.call-done = bf16[2048,1024]{1,0:T(8,128)(2,1)} async-done(((bf16[512,1024]{1,0:T(8,128)(2,1)}), bf16[2048,1024]{1,0:T(8,128)(2,1)}) %all-gather.28.cloned.1.call-update) | async-done | bytes 4194320 | tf_op jit(solution)/shard_map/all_gather | solution.py:60
  632.8 44.7 %all-gather.26.cloned.1.call-done = bf16[2048,1024]{1,0:T(8,128)(2,1)} async-done(((bf16[512,1024]{1,0:T(8,128)(2,1)}), bf16[2048,1024]{1,0:T(8,128)(2,1)}) %all-gather.26.cloned.1.call-update) | async-done | bytes 4194320 | tf_op jit(solution)/shard_map/all_gather | solution.py:59
  687.5 44.4 %all-gather.30.cloned.1.call-done = bf16[2048,1024]{1,0:T(8,128)(2,1)} async-done(((bf16[512,1024]{1,0:T(8,128)(2,1)}), bf16[2048,1024]{1,0:T(8,128)(2,1)}) %all-gather.30.cloned.1.call-update) | async-done | bytes 4194320 | tf_op jit(solution)/shard_map/all_gather | solution.py:61
  731.9 49.4 %all-gather.36.cloned.1.call-done = bf16[1,1024,2048]{2,1,0:T(8,128)(2,1)} async-done(((bf16[1,128,2048]{2,1,0:T(8,128)(2,1)}), bf16[1,1024,2048]{2,1,0:T(8,128)(2,1)}) %all-gather.36.cloned.1.call-update) | async-done | bytes 4194320 | tf_op jit(solution)/shard_map/all_gather | solution.py:235
  781.3 13.2 multiply_convert_fusion.6
  813.7 15.5 all-gather.34.cloned.1.call-done
  922.4 273.4 %all-reduce.17.cloned.1.call-done = (f32[1024,2048]{1,0:T(8,128)}, f32[1024,2048]{1,0:T(8,128)}) async-done(((f32[1024,2048]{1,0:T(8,128)}, f32[1024,2048]{1,0:T(8,128)}), (f32[1024,2048]{1,0:T(8,128)}, f32[1024,2048]{1,0:T(8,128)})) %all-reduce.17.cloned.1.call-update) | async-done | bytes 16777232 | tf_op jit(solution)/shard_map/psum | solution.py:247
  1195.8 14.5 select_reduce_fusion.1
  1210.4 22.6 %multiply_add_fusion.1 = (f32[1024,2048]{1,0:T(8,128)}, f32[1024,2048]{1,0:T(8,128)}) fusion(f32[1024,2048]{1,0:T(8,128)} %get-tuple-element.50, f32[1024,2048]{1,0:T(8,128)} %get-tuple-element.52, bf16[1,1024,2048]{2,1,0:T(8,128)(2,1)} %all-gather.34.cloned.1.call-done, f32[1024]{0:T(1024)S(1)} %broadcast_multiply_fusion.1, f32[2048]{0:T(1024)S(1)} %bitcast.256, ...), kind=kLoop, calls=%fused_computation.21 | loop fusion | flops 29360128 | bytes 58744832 | tf_op jit(solution)/shard_map/add | solution.py:250
  1370.4 44.7 %reduce-scatter.12.cloned.1.call-done = bf16[128,2048]{1,0:T(8,128)(2,1)} async-done(((bf16[1024,2048]{1,0:T(8,128)(2,1)}), bf16[128,2048]{1,0:T(8,128)(2,1)}) %reduce-scatter.12.cloned.1.call-update) | async-done | bytes 524304 | tf_op jit(solution)/shard_map/reduce_scatter | solution.py:230
  1416.6 48.9 %reduce-scatter.14.cloned.1.call-done = bf16[128,2048]{1,0:T(8,128)(2,1)} async-done(((bf16[1024,2048]{1,0:T(8,128)(2,1)}), bf16[128,2048]{1,0:T(8,128)(2,1)}) %reduce-scatter.14.cloned.1.call-update) | async-done | bytes 524304 | tf_op jit(solution)/shard_map/reduce_scatter | solution.py:230
  1468.1 26.5 %reduce-scatter.26.cloned.1.call-done = bf16[512,256]{1,0:T(8,128)(2,1)} async-done(((bf16[2048,256]{1,0:T(8,128)(2,1)}), bf16[512,256]{1,0:T(8,128)(2,1)}) %reduce-scatter.26.cloned.1.call-update) | async-done | bytes 262160 | tf_op jit(solution)/shard_map/reduce_scatter | solution.py:79
  1496.3 28.7 %reduce-scatter.24.cloned.1.call-done = bf16[512,256]{1,0:T(8,128)(2,1)} async-done(((bf16[2048,256]{1,0:T(8,128)(2,1)}), bf16[512,256]{1,0:T(8,128)(2,1)}) %reduce-scatter.24.cloned.1.call-update) | async-done | bytes 262160 | tf_op jit(solution)/shard_map/reduce_scatter | solution.py:76
  1526.8 29.1 %reduce-scatter.22.cloned.1.call-done = bf16[512,256]{1,0:T(8,128)(2,1)} async-done(((bf16[2048,256]{1,0:T(8,128)(2,1)}), bf16[512,256]{1,0:T(8,128)(2,1)}) %reduce-scatter.22.cloned.1.call-update) | async-done | bytes 262160 | tf_op jit(solution)/shard_map/reduce_scatter | solution.py:73
  1557.7 29.4 %reduce-scatter.20.cloned.1.call-done = bf16[512,256]{1,0:T(8,128)(2,1)} async-done(((bf16[2048,256]{1,0:T(8,128)(2,1)}), bf16[512,256]{1,0:T(8,128)(2,1)}) %reduce-scatter.20.cloned.1.call-update) | async-done | bytes 262160 | tf_op jit(solution)/shard_map/reduce_scatter | solution.py:70
  1589.0 50.6 %reduce-scatter.18.cloned.1.call-done = bf16[128,2048]{1,0:T(8,128)(2,1)} async-done(((bf16[1024,2048]{1,0:T(8,128)(2,1)}), bf16[128,2048]{1,0:T(8,128)(2,1)}) %reduce-scatter.18.cloned.1.call-update) | async-done | bytes 524304 | tf_op jit(solution)/shard_map/reduce_scatter | solution.py:279
  1639.6 50.4 %reduce-scatter.16.cloned.1.call-done = bf16[128,2048]{1,0:T(8,128)(2,1)} async-done(((bf16[1024,2048]{1,0:T(8,128)(2,1)}), bf16[128,2048]{1,0:T(8,128)(2,1)}) %reduce-scatter.16.cloned.1.call-update) | async-done | bytes 524304 | tf_op jit(solution)/shard_map/reduce_scatter | solution.py:279
  1692.0 25.9 %all-reduce.10 = (bf16[2048]{0:T(1024)(128)(2,1)S(1)}, bf16[2048]{0:T(1024)(128)(2,1)S(1)}) all-reduce(f32[2048]{0:T(1024)S(1)} %add.306, f32[2048]{0:T(1024)S(1)} %add.308), channel_id=1, replica_groups=mesh['batch'=4,'head'=8] {'head'}, use_global_device_ids=true, to_apply=%region_37.38 | all-reduce | flops 4096 | bytes 24576 | tf_op jit(solution)/shard_map/psum | solution.py:68
  (487 shorter events, 421.2 us)
Async XLA Ops:
  7.2 32.0 %all-gather.22.cloned.1.call-start = ((), (), s32[]{:S(2)}) async-start(), calls=%async_computation.14 | async-start | bytes 1310720 | tf_op jit(solution)/shard_map/all_gather | solution.py:56
  7.9 80.7 %all-gather.32.cloned.1.call-start = ((), (), s32[]{:S(2)}) async-start(), calls=%async_computation.20 | async-start | bytes 4718592 | tf_op jit(solution)/shard_map/all_gather | solution.py:200
  22.3 93.5 %all-gather.20.cloned.1.call-start = ((), (), s32[]{:S(2)}) async-start(), calls=%async_computation.13 | async-start | bytes 1310720 | tf_op jit(solution)/shard_map/all_gather | solution.py:55
  23.0 121.1 %all-gather.18.cloned.1.call-start = ((), (), s32[]{:S(2)}) async-start(), calls=%async_computation.12 | async-start | bytes 1310720 | tf_op jit(solution)/shard_map/all_gather | solution.py:57
  23.6 169.7 %all-gather.16.cloned.1.call-start = ((), (), s32[]{:S(2)}) async-start(), calls=%async_computation.11 | async-start | bytes 4718592 | tf_op jit(solution)/shard_map/all_gather | solution.py:200
  24.2 196.5 %all-gather.24.cloned.1.call-start = ((), (), s32[]{:S(2)}) async-start(), calls=%async_computation.15 | async-start | bytes 1310720 | tf_op jit(solution)/shard_map/all_gather | solution.py:58
  24.8 543.4 %all-reduce.19.cloned.1.call-start = ((), (), s32[]{:S(2)}) async-start(), calls=%async_computation.34 | async-start | bytes 33554432 | tf_op jit(solution)/shard_map/psum | solution.py:223
  234.5 388.4 %all-gather.28.cloned.1.call-start = ((), (), s32[]{:S(2)}) async-start(), calls=%async_computation.17 | async-start | bytes 5242880 | tf_op jit(solution)/shard_map/all_gather | solution.py:60
  235.2 442.3 %all-gather.26.cloned.1.call-start = ((), (), s32[]{:S(2)}) async-start(), calls=%async_computation.16 | async-start | bytes 5242880 | tf_op jit(solution)/shard_map/all_gather | solution.py:59
  236.0 495.9 %all-gather.30.cloned.1.call-start = ((), (), s32[]{:S(2)}) async-start(), calls=%async_computation.18 | async-start | bytes 5242880 | tf_op jit(solution)/shard_map/all_gather | solution.py:61
  236.5 544.7 %all-gather.36.cloned.1.call-start = ((), (), s32[]{:S(2)}) async-start(), calls=%async_computation.32 | async-start | bytes 4718592 | tf_op jit(solution)/shard_map/all_gather | solution.py:235
  237.7 591.5 %all-gather.34.cloned.1.call-start = ((), (), s32[]{:S(2)}) async-start(), calls=%async_computation.31 | async-start | bytes 4718592 | tf_op jit(solution)/shard_map/all_gather | solution.py:235
  238.2 957.6 %all-reduce.17.cloned.1.call-start = ((), (), s32[]{:S(2)}) async-start(), calls=%async_computation.33 | async-start | bytes 33554432 | tf_op jit(solution)/shard_map/psum | solution.py:247
  863.4 498.8 %reduce-scatter.32.cloned.1.call-start = ((), (), s32[]{:S(2)}) async-start(), calls=%async_computation.30 | async-start | bytes 5242880 | tf_op jit(solution)/shard_map/reduce_scatter | solution.py:88
  876.4 488.4 %reduce-scatter.30.cloned.1.call-start = ((), (), s32[]{:S(2)}) async-start(), calls=%async_computation.29 | async-start | bytes 5242880 | tf_op jit(solution)/shard_map/reduce_scatter | solution.py:85
  889.9 477.7 %reduce-scatter.28.cloned.1.call-start = ((), (), s32[]{:S(2)}) async-start(), calls=%async_computation.28 | async-start | bytes 5242880 | tf_op jit(solution)/shard_map/reduce_scatter | solution.py:82
  903.6 511.5 %reduce-scatter.12.cloned.1.call-start = ((), (), s32[]{:S(2)}) async-start(), calls=%async_computation.19 | async-start | bytes 4718592 | tf_op jit(solution)/shard_map/reduce_scatter | solution.py:230
  913.1 552.4 %reduce-scatter.14.cloned.1.call-start = ((), (), s32[]{:S(2)}) async-start(), calls=%async_computation.21 | async-start | bytes 4718592 | tf_op jit(solution)/shard_map/reduce_scatter | solution.py:230
  922.3 572.2 %reduce-scatter.26.cloned.1.call-start = ((), (), s32[]{:S(2)}) async-start(), calls=%async_computation.27 | async-start | bytes 1310720 | tf_op jit(solution)/shard_map/reduce_scatter | solution.py:79
  1303.9 221.2 %reduce-scatter.24.cloned.1.call-start = ((), (), s32[]{:S(2)}) async-start(), calls=%async_computation.26 | async-start | bytes 1310720 | tf_op jit(solution)/shard_map/reduce_scatter | solution.py:76
  1326.7 229.3 %reduce-scatter.22.cloned.1.call-start = ((), (), s32[]{:S(2)}) async-start(), calls=%async_computation.25 | async-start | bytes 1310720 | tf_op jit(solution)/shard_map/reduce_scatter | solution.py:73
  1339.5 247.6 %reduce-scatter.20.cloned.1.call-start = ((), (), s32[]{:S(2)}) async-start(), calls=%async_computation.24 | async-start | bytes 1310720 | tf_op jit(solution)/shard_map/reduce_scatter | solution.py:70
  1346.3 293.3 %reduce-scatter.18.cloned.1.call-start = ((), (), s32[]{:S(2)}) async-start(), calls=%async_computation.23 | async-start | bytes 4718592 | tf_op jit(solution)/shard_map/reduce_scatter | solution.py:279
  1352.8 337.3 %reduce-scatter.16.cloned.1.call-start = ((), (), s32[]{:S(2)}) async-start(), calls=%async_computation.22 | async-start | bytes 4718592 | tf_op jit(solution)/shard_map/reduce_scatter | solution.py:279
  (145 other events, 3505.5 us)
Sparse Core Ops, SparseCore 0:
  9.9 29.3 all-gather.21
  41.4 47.1 all-gather.31
  90.4 25.3 all-gather.19
  117.5 26.6 all-gather.17
  146.2 47.0 all-gather.15
  195.0 25.7 all-gather.23
  234.6 333.5 all-reduce.18
  570.0 52.7 all-gather.27
  624.7 52.6 all-gather.25
  679.2 52.6 all-gather.29
  734.1 47.1 all-gather.35
  783.3 45.8 all-gather.33
  863.5 332.2 all-reduce.16
  1198.6 52.7 reduce-scatter.31
  1254.5 52.6 reduce-scatter.29
  1310.1 52.6 reduce-scatter.27
  1365.0 49.9 reduce-scatter.11
  1417.3 48.1 reduce-scatter.13
  1468.6 25.8 reduce-scatter.25
  1497.3 27.7 reduce-scatter.23
  1528.2 27.7 reduce-scatter.21
  1559.4 27.7 reduce-scatter.19
  1589.6 49.9 reduce-scatter.17
  1641.9 48.1 reduce-scatter.15
where the time goes:
time: 1740 us
  waiting for transfers between devices  1240 us (71%)
  matrix products  291 us (17%)
  other arithmetic  115 us (7%)
  blocking collectives  53.5 us (3%)
  local copies, waits for them, and re-layouts  26.5 us (2%)
    psum x1, waiting for transfers between devices, per_device(): mixed_full = lax.psum(attn_terms + placed, 'head')  322 us
    psum x1, waiting for transfers between devices, per_device(): grad_mlp_in = lax.psum(mlp_in_terms, 'head')  273 us
    reduce_scatter x2, waiting for transfers between devices, per_device(): lax.psum_scatter(attn_in_terms.astype(jnp.bfloat16), 'head', scatter_dime...  101 us
    reduce_scatter x2, waiting for transfers between devices, per_device(): lax.psum_scatter(mlp_terms.astype(jnp.bfloat16), 'head', scatter_dimensio...  93.6 us
    all_gather x2, waiting for transfers between devices, per_device(): lax.all_gather(normed(inputs, gain_one).astype(jnp.bfloat16), 'head', axi...  74.6 us
    dot_general x14, matrix products, contract_cols(): lax.dot_general(left, right, (((1,), (1,)), ((), ())), preferred_element_...  69.3 us
    all_gather x2, waiting for transfers between devices, per_device(): grad_full = lax.all_gather(grad_row, 'head', axis=0, tiled=True)  64.9 us
    dot_general x14, matrix products, contract_rows(): lax.dot_general(left, right, (((0,), (0,)), ((), ())), preferred_element_...  57.6 us
  transfers between devices with their start and end apart: 24, of which 21 were waited for; matrix products, arithmetic and copies ran while one was open for 20% of the time, Pallas kernels for 0%

commit v1 on v0

--- a/solution.py
+++ b/solution.py
@@ -7,6 +7,22 @@
 epsilon = 1e-05
 rope_base = 130000.0
 masked_value = -1000000000.0
+
+
+def ring_gather(x, axis, dim):
+    ways, here, hop = (lax.axis_size(axis), lax.axis_index(axis), x.shape[dim])
+    dims = [n * ways if d == dim else n for d, n in enumerate(x.shape)]
+    full = lax.dynamic_update_slice_in_dim(jnp.zeros(dims, x.dtype), x, here * hop, axis=dim)
+    going_up = going_down = x
+    for far in range(1, ways // 2 + 1):
+        going_up = lax.ppermute(going_up, axis, [(d, (d + 1) % ways) for d in range(ways)])
+        full = lax.dynamic_update_slice_in_dim(full, going_up, (here - far) % ways * hop, axis=dim)
+        if 2 * far < ways:
+            going_down = lax.ppermute(going_down, axis, [(d, (d - 1) % ways) for d in range(ways)])
+            full = lax.dynamic_update_slice_in_dim(
+                full, going_down, (here + far) % ways * hop, axis=dim
+            )
+    return full
 
 
 def normed(values, gain):
@@ -197,9 +213,7 @@
         segments = segment_ids[row_index]
         cosine, sine = rope_tables(position_ids[row_index])
         inputs = tokens[row_index].astype(jnp.float32)
-        attn_in = lax.all_gather(
-            normed(inputs, gain_one).astype(jnp.bfloat16), "head", axis=0, tiled=True
-        )
+        attn_in = ring_gather(normed(inputs, gain_one).astype(jnp.bfloat16), "head", 0)
         length = attn_in.shape[0]
         heads_here = query_w.shape[1] // HEAD_DIM
         head_shape = (length, heads_here, HEAD_DIM)

time: 1740 us -> 1690 us (0.971)
  waiting for transfers between devices: 1240 us -> 1150 us
  starting transfers between devices: 1.43 us -> 23.3 us
  local copies, waits for them, and re-layouts: 26.5 us -> 47.2 us
    all_gather x2 -> x0, waiting for transfers between devices: 74.6 us -> none  [per_device(): lax.all_gather(normed(inputs, gain_one).astype(jnp.bfloat16), 'head', axi...]
    ppermute x0 -> x14, waiting for transfers between devices: none -> 40.8 us  [the longest x8 36.9 us: ring_gather(): lax.ppermute(going_up, axis, [(d, (d + 1) % ways) for d in range(ways)])]
    all_gather x1, waiting for transfers between devices: 23.4 us -> 0.02 us  [fetch_weights(): lax.all_gather(w_query, 'batch', axis=0, tiled=True)]
    ppermute x0 -> x14, starting transfers between devices: none -> 21.9 us  [the longest x6 21.6 us: ring_gather(): lax.ppermute(going_down, axis, [(d, (d - 1) % ways) for d in range(ways)])]
  transfers between devices with their start and end apart: 24 -> 36, of which waited for: 21 -> 25; matrix products, arithmetic and copies ran while one was open for 20% -> 22% of each run, Pallas kernels for 0% -> 0%
where the time goes in v1:
time: 1690 us; the launch traced here: 1680 us
  waiting for transfers between devices  1150 us (68%)
  matrix products  286 us (17%)
  other arithmetic  107 us (6%)
  blocking collectives  53.5 us (3%)
  local copies, waits for them, and re-layouts  47.2 us (3%)
  starting transfers between devices  23.3 us (1%)
  between operations  17.8 us (1%)
    psum x1, waiting for transfers between devices, per_device(): mixed_full = lax.psum(attn_terms + placed, 'head')  320 us
    psum x1, waiting for transfers between devices, per_device(): grad_mlp_in = lax.psum(mlp_in_terms, 'head')  273 us
    reduce_scatter x2, waiting for transfers between devices, per_device(): lax.psum_scatter(attn_in_terms.astype(jnp.bfloat16), 'head', scatter_dime...  101 us
    reduce_scatter x2, waiting for transfers between devices, per_device(): lax.psum_scatter(mlp_terms.astype(jnp.bfloat16), 'head', scatter_dimensio...  98.4 us
    dot_general x14, matrix products, contract_cols(): lax.dot_general(left, right, (((1,), (1,)), ((), ())), preferred_element_...  69.9 us
    dot_general x14, matrix products, contract_rows(): lax.dot_general(left, right, (((0,), (0,)), ((), ())), preferred_element_...  69.4 us
    all_gather x2, waiting for transfers between devices, per_device(): grad_full = lax.all_gather(grad_row, 'head', axis=0, tiled=True)  64.5 us
    all_gather x1, waiting for transfers between devices, fetch_weights(): lax.all_gather(w_down, 'batch', axis=0, tiled=True)  44.6 us
  transfers between devices with their start and end apart: 36, of which 25 were waited for; matrix products, arithmetic and copies ran while one was open for 22% of the time, Pallas kernels for 0%

profile of v1, /device:TPU:0, one launch (start us, length us, event | category | flops | bytes accessed | tf_op | source)
XLA Modules:
  0.0 1684.8 jit_solution(16626932488229071046)
XLA Ops:
  84.0 11.1 collective-permute-done.11
  192.2 320.3 %all-reduce.19.cloned.1.call-done = (f32[1024,2048]{1,0:T(8,128)}, f32[1024,2048]{1,0:T(8,128)}) async-done(((f32[1024,2048]{1,0:T(8,128)}, f32[1024,2048]{1,0:T(8,128)}), (f32[1024,2048]{1,0:T(8,128)}, f32[1024,2048]{1,0:T(8,128)})) %all-reduce.19.cloned.1.call-update) | async-done | bytes 16777232 | tf_op jit(solution)/shard_map/psum | solution.py:237
  525.3 41.7 %all-gather.24.cloned.1.call-done = bf16[2048,1024]{1,0:T(8,128)(2,1)} async-done(((bf16[512,1024]{1,0:T(8,128)(2,1)}), bf16[2048,1024]{1,0:T(8,128)(2,1)}) %all-gather.24.cloned.1.call-update) | async-done | bytes 4194320 | tf_op jit(solution)/shard_map/all_gather | solution.py:76
  567.0 9.9 fusion.155
  577.0 44.6 %all-gather.22.cloned.1.call-done = bf16[2048,1024]{1,0:T(8,128)(2,1)} async-done(((bf16[512,1024]{1,0:T(8,128)(2,1)}), bf16[2048,1024]{1,0:T(8,128)(2,1)}) %all-gather.22.cloned.1.call-update) | async-done | bytes 4194320 | tf_op jit(solution)/shard_map/all_gather | solution.py:75
  621.6 9.9 fusion.154
  631.5 44.6 %all-gather.26.cloned.1.call-done = bf16[2048,1024]{1,0:T(8,128)(2,1)} async-done(((bf16[512,1024]{1,0:T(8,128)(2,1)}), bf16[2048,1024]{1,0:T(8,128)(2,1)}) %all-gather.26.cloned.1.call-update) | async-done | bytes 4194320 | tf_op jit(solution)/shard_map/all_gather | solution.py:77
  676.2 49.4 %all-gather.30.cloned.1.call-done = bf16[1,1024,2048]{2,1,0:T(8,128)(2,1)} async-done(((bf16[1,128,2048]{2,1,0:T(8,128)(2,1)}), bf16[1,1024,2048]{2,1,0:T(8,128)(2,1)}) %all-gather.30.cloned.1.call-update) | async-done | bytes 4194320 | tf_op jit(solution)/shard_map/all_gather | solution.py:249
  725.6 13.3 multiply_convert_fusion.6
  758.3 15.1 all-gather.28.cloned.1.call-done
  773.5 13.2 multiply_convert_fusion.7
  866.7 273.4 %all-reduce.17.cloned.1.call-done = (f32[1024,2048]{1,0:T(8,128)}, f32[1024,2048]{1,0:T(8,128)}) async-done(((f32[1024,2048]{1,0:T(8,128)}, f32[1024,2048]{1,0:T(8,128)}), (f32[1024,2048]{1,0:T(8,128)}, f32[1024,2048]{1,0:T(8,128)})) %all-reduce.17.cloned.1.call-update) | async-done | bytes 16777232 | tf_op jit(solution)/shard_map/psum | solution.py:261
  1140.0 14.7 select_reduce_fusion.1
  1154.8 22.6 %multiply_add_fusion.1 = (f32[1024,2048]{1,0:T(8,128)}, f32[1024,2048]{1,0:T(8,128)}) fusion(f32[1024,2048]{1,0:T(8,128)} %get-tuple-element.50, f32[1024,2048]{1,0:T(8,128)} %get-tuple-element.52, bf16[1,1024,2048]{2,1,0:T(8,128)(2,1)} %all-gather.28.cloned.1.call-done, f32[1024]{0:T(1024)S(1)} %broadcast_multiply_fusion.1, f32[2048]{0:T(1024)S(1)} %bitcast.259, ...), kind=kLoop, calls=%fused_computation.21 | loop fusion | flops 29360128 | bytes 58744832 | tf_op jit(solution)/shard_map/add | solution.py:264
  1310.0 49.5 %reduce-scatter.12.cloned.1.call-done = bf16[128,2048]{1,0:T(8,128)(2,1)} async-done(((bf16[1024,2048]{1,0:T(8,128)(2,1)}), bf16[128,2048]{1,0:T(8,128)(2,1)}) %reduce-scatter.12.cloned.1.call-update) | async-done | bytes 524304 | tf_op jit(solution)/shard_map/reduce_scatter | solution.py:244
  1361.0 48.9 %reduce-scatter.14.cloned.1.call-done = bf16[128,2048]{1,0:T(8,128)(2,1)} async-done(((bf16[1024,2048]{1,0:T(8,128)(2,1)}), bf16[128,2048]{1,0:T(8,128)(2,1)}) %reduce-scatter.14.cloned.1.call-update) | async-done | bytes 524304 | tf_op jit(solution)/shard_map/reduce_scatter | solution.py:244
  1412.5 26.3 %reduce-scatter.26.cloned.1.call-done = bf16[512,256]{1,0:T(8,128)(2,1)} async-done(((bf16[2048,256]{1,0:T(8,128)(2,1)}), bf16[512,256]{1,0:T(8,128)(2,1)}) %reduce-scatter.26.cloned.1.call-update) | async-done | bytes 262160 | tf_op jit(solution)/shard_map/reduce_scatter | solution.py:95
  1440.6 28.7 %reduce-scatter.24.cloned.1.call-done = bf16[512,256]{1,0:T(8,128)(2,1)} async-done(((bf16[2048,256]{1,0:T(8,128)(2,1)}), bf16[512,256]{1,0:T(8,128)(2,1)}) %reduce-scatter.24.cloned.1.call-update) | async-done | bytes 262160 | tf_op jit(solution)/shard_map/reduce_scatter | solution.py:92
  1471.1 29.1 %reduce-scatter.22.cloned.1.call-done = bf16[512,256]{1,0:T(8,128)(2,1)} async-done(((bf16[2048,256]{1,0:T(8,128)(2,1)}), bf16[512,256]{1,0:T(8,128)(2,1)}) %reduce-scatter.22.cloned.1.call-update) | async-done | bytes 262160 | tf_op jit(solution)/shard_map/reduce_scatter | solution.py:89
  1502.0 29.3 %reduce-scatter.20.cloned.1.call-done = bf16[512,256]{1,0:T(8,128)(2,1)} async-done(((bf16[2048,256]{1,0:T(8,128)(2,1)}), bf16[512,256]{1,0:T(8,128)(2,1)}) %reduce-scatter.20.cloned.1.call-update) | async-done | bytes 262160 | tf_op jit(solution)/shard_map/reduce_scatter | solution.py:86
  1533.1 50.7 %reduce-scatter.18.cloned.1.call-done = bf16[128,2048]{1,0:T(8,128)(2,1)} async-done(((bf16[1024,2048]{1,0:T(8,128)(2,1)}), bf16[128,2048]{1,0:T(8,128)(2,1)}) %reduce-scatter.18.cloned.1.call-update) | async-done | bytes 524304 | tf_op jit(solution)/shard_map/reduce_scatter | solution.py:293
  1583.7 50.6 %reduce-scatter.16.cloned.1.call-done = bf16[128,2048]{1,0:T(8,128)(2,1)} async-done(((bf16[1024,2048]{1,0:T(8,128)(2,1)}), bf16[128,2048]{1,0:T(8,128)(2,1)}) %reduce-scatter.16.cloned.1.call-update) | async-done | bytes 524304 | tf_op jit(solution)/shard_map/reduce_scatter | solution.py:293
  1636.3 25.9 %all-reduce.10 = (bf16[2048]{0:T(1024)(128)(2,1)S(1)}, bf16[2048]{0:T(1024)(128)(2,1)S(1)}) all-reduce(f32[2048]{0:T(1024)S(1)} %add.398, f32[2048]{0:T(1024)S(1)} %add.400), channel_id=1, replica_groups=mesh['batch'=4,'head'=8] {'head'}, use_global_device_ids=true, to_apply=%region_37.38 | all-reduce | flops 4096 | bytes 24576 | tf_op jit(solution)/shard_map/psum | solution.py:84
  1662.2 10.0 all-reduce.13
  (538 shorter events, 433.9 us)
Async XLA Ops:
  7.2 102.2 %all-gather.18.cloned.1.call-start = ((), (), s32[]{:S(2)}) async-start(), calls=%async_computation.13 | async-start | bytes 1310720 | tf_op jit(solution)/shard_map/all_gather | solution.py:72
  7.9 105.2 %all-gather.16.cloned.1.call-start = ((), (), s32[]{:S(2)}) async-start(), calls=%async_computation.12 | async-start | bytes 1310720 | tf_op jit(solution)/shard_map/all_gather | solution.py:71
  8.7 118.5 %all-gather.14.cloned.1.call-start = ((), (), s32[]{:S(2)}) async-start(), calls=%async_computation.11 | async-start | bytes 1310720 | tf_op jit(solution)/shard_map/all_gather | solution.py:73
  9.4 156.9 %all-gather.20.cloned.1.call-start = ((), (), s32[]{:S(2)}) async-start(), calls=%async_computation.14 | async-start | bytes 1310720 | tf_op jit(solution)/shard_map/all_gather | solution.py:74
  35.6 476.8 %all-reduce.19.cloned.1.call-start = ((), (), s32[]{:S(2)}) async-start(), calls=%async_computation.32 | async-start | bytes 33554432 | tf_op jit(solution)/shard_map/psum | solution.py:237
  63.5 34.6 %collective-permute-start.5 = (bf16[128,2048]{1,0:T(8,128)(2,1)S(1)}, bf16[128,2048]{1,0:T(8,128)(2,1)S(1)}, u32[]{:S(2)}, u32[]{:S(2)}) collective-permute-start(bf16[128,2048]{1,0:T(8,128)(2,1)S(1)} %collective-permute-done.3), channel_id=1, source_target_pairs={{0,7},{1,0},{2,1},{3,2},{4,3},{5,4},{6,5},{7,6},{8,15},{9,8},{10,9... | collective-permute-start | bytes 1572872 | tf_op jit(solution)/shard_map/ppermute | solution.py:21
  83.9 54.9 %collective-permute-start.6 = (bf16[128,2048]{1,0:T(8,128)(2,1)}, bf16[128,2048]{1,0:T(8,128)(2,1)}, u32[]{:S(2)}, u32[]{:S(2)}) collective-permute-start(bf16[128,2048]{1,0:T(8,128)(2,1)} %collective-permute-done.4), channel_id=1, source_target_pairs={{0,1},{1,2},{2,3},{3,4},{4,5},{5,6},{6,7},{7,0},{8,9},{9,10},{10,1... | collective-permute-start | bytes 1572872 | tf_op jit(solution)/shard_map/ppermute | solution.py:18
  180.2 386.8 %all-gather.24.cloned.1.call-start = ((), (), s32[]{:S(2)}) async-start(), calls=%async_computation.16 | async-start | bytes 5242880 | tf_op jit(solution)/shard_map/all_gather | solution.py:76
  180.8 440.8 %all-gather.22.cloned.1.call-start = ((), (), s32[]{:S(2)}) async-start(), calls=%async_computation.15 | async-start | bytes 5242880 | tf_op jit(solution)/shard_map/all_gather | solution.py:75
  181.6 494.6 %all-gather.26.cloned.1.call-start = ((), (), s32[]{:S(2)}) async-start(), calls=%async_computation.17 | async-start | bytes 5242880 | tf_op jit(solution)/shard_map/all_gather | solution.py:77
  182.3 543.3 %all-gather.30.cloned.1.call-start = ((), (), s32[]{:S(2)}) async-start(), calls=%async_computation.30 | async-start | bytes 4718592 | tf_op jit(solution)/shard_map/all_gather | solution.py:249
  183.4 590.0 %all-gather.28.cloned.1.call-start = ((), (), s32[]{:S(2)}) async-start(), calls=%async_computation.29 | async-start | bytes 4718592 | tf_op jit(solution)/shard_map/all_gather | solution.py:249
  184.0 956.0 %all-reduce.17.cloned.1.call-start = ((), (), s32[]{:S(2)}) async-start(), calls=%async_computation.31 | async-start | bytes 33554432 | tf_op jit(solution)/shard_map/psum | solution.py:261
  807.5 492.3 %reduce-scatter.32.cloned.1.call-start = ((), (), s32[]{:S(2)}) async-start(), calls=%async_computation.28 | async-start | bytes 5242880 | tf_op jit(solution)/shard_map/reduce_scatter | solution.py:104
  820.5 481.9 %reduce-scatter.30.cloned.1.call-start = ((), (), s32[]{:S(2)}) async-start(), calls=%async_computation.27 | async-start | bytes 5242880 | tf_op jit(solution)/shard_map/reduce_scatter | solution.py:101
  834.0 473.2 %reduce-scatter.28.cloned.1.call-start = ((), (), s32[]{:S(2)}) async-start(), calls=%async_computation.26 | async-start | bytes 5242880 | tf_op jit(solution)/shard_map/reduce_scatter | solution.py:98
  847.7 511.7 %reduce-scatter.12.cloned.1.call-start = ((), (), s32[]{:S(2)}) async-start(), calls=%async_computation.18 | async-start | bytes 4718592 | tf_op jit(solution)/shard_map/reduce_scatter | solution.py:244
  857.4 552.4 %reduce-scatter.14.cloned.1.call-start = ((), (), s32[]{:S(2)}) async-start(), calls=%async_computation.19 | async-start | bytes 4718592 | tf_op jit(solution)/shard_map/reduce_scatter | solution.py:244
  866.6 572.2 %reduce-scatter.26.cloned.1.call-start = ((), (), s32[]{:S(2)}) async-start(), calls=%async_computation.25 | async-start | bytes 1310720 | tf_op jit(solution)/shard_map/reduce_scatter | solution.py:95
  1233.9 235.4 %reduce-scatter.24.cloned.1.call-start = ((), (), s32[]{:S(2)}) async-start(), calls=%async_computation.24 | async-start | bytes 1310720 | tf_op jit(solution)/shard_map/reduce_scatter | solution.py:92
  1257.1 243.1 %reduce-scatter.22.cloned.1.call-start = ((), (), s32[]{:S(2)}) async-start(), calls=%async_computation.23 | async-start | bytes 1310720 | tf_op jit(solution)/shard_map/reduce_scatter | solution.py:89
  1273.8 257.5 %reduce-scatter.20.cloned.1.call-start = ((), (), s32[]{:S(2)}) async-start(), calls=%async_computation.22 | async-start | bytes 1310720 | tf_op jit(solution)/shard_map/reduce_scatter | solution.py:86
  1284.1 299.6 %reduce-scatter.18.cloned.1.call-start = ((), (), s32[]{:S(2)}) async-start(), calls=%async_computation.21 | async-start | bytes 4718592 | tf_op jit(solution)/shard_map/reduce_scatter | solution.py:293
  1290.4 343.9 %reduce-scatter.16.cloned.1.call-start = ((), (), s32[]{:S(2)}) async-start(), calls=%async_computation.20 | async-start | bytes 4718592 | tf_op jit(solution)/shard_map/reduce_scatter | solution.py:293
  (163 other events, 3547.7 us)
Sparse Core Ops, SparseCore 0:
  9.9 29.3 all-gather.17
  41.1 26.6 all-gather.15
  69.6 26.6 all-gather.13
  97.9 26.6 all-gather.19
  180.3 332.1 all-reduce.18
  514.2 52.8 all-gather.23
  568.9 52.6 all-gather.21
  623.4 52.6 all-gather.25
  678.4 47.1 all-gather.29
  727.6 45.8 all-gather.27
  807.7 332.3 all-reduce.16
  1142.8 52.7 reduce-scatter.31
  1198.9 52.6 reduce-scatter.29
  1254.4 52.6 reduce-scatter.27
  1309.4 49.9 reduce-scatter.11
  1361.7 48.1 reduce-scatter.13
  1412.9 25.8 reduce-scatter.25
  1441.5 27.7 reduce-scatter.23
  1472.4 27.7 reduce-scatter.21
  1503.5 27.7 reduce-scatter.19
  1533.7 49.9 reduce-scatter.17
  1586.1 48.1 reduce-scatter.15
